TPU v7x, 256 devices: a whole 4x4x8 slice. The times are simulated.
256 devices in a mesh: blk: 64 (over z, y, core), col: 4 (over x).
Axes of the slice: x: 4, y: 4, z: 8, core: 2. Of those that a mesh axis runs over, the one named last changes fastest.
Arguments:
- y_start: float32 [128, 131072], P('col', 'blk')
- tile_real: bfloat16 [6144, 256, 256], P('blk'), may hold values from 0 to 1, as said below
- tile_imag: bfloat16 [6144, 256, 256], P('blk'), may hold values from -1 to 1, as said below
- tile_rows: int32 [6144], P('blk'), may hold values from 0 to 7
- tile_slots: int32 [6144], P('blk'), may hold values from 0 to 71, as said below
- fetch_pick: int32 [64, 64], P('blk'), may hold values from 0 to 7
Outputs:
- encodings: float32 [128, 131072], P('col', 'blk')
Inputs may be any that keep to these rules, and one draw needn't show every extreme that they name: `tile_slots`: on each device the first 16 of its 96 tiles name an own row block (0 to 7); the others name 8 + p for an owning device p other than itself; every device reads from the devices 1, 32 and -1 places away along blk, modulo the axis. `tile_real`: entries are 0 or 1. `tile_imag`: entries are -1, 0 or 1, and never nonzero where tile_real is nonzero.
All inputs are finite; a program needn't handle non-finite values.
Results may differ from a plain program's by a relative error of at most 0.0031.
Values may be sent and summed in bfloat16 or wider, within the bound.
A program may use at most 128 MiB of HBM per device.

v0:
```python
import math

import jax
import jax.numpy as jnp
from jax import lax
from jax.sharding import PartitionSpec as P

LOC_RB = 2
STEPS = 4


center = 1.25
half_width = 0.75


def turn(values):
    pairs = values.reshape((values.shape[0] // 2, 2) + values.shape[1:])
    return jnp.stack([-pairs[:, 1], pairs[:, 0]], axis=1).reshape(values.shape)


def tile_products(picked, real_part, imag_part, member):
    prod_re = jnp.einsum("ctb,tab->cta", picked, real_part, preferred_element_type=jnp.float32)
    prod_im = jnp.einsum("ctb,tab->cta", picked, imag_part, preferred_element_type=jnp.float32)
    sum_re = jnp.einsum("cta,tr->cra", prod_re, member, precision=lax.Precision.HIGHEST)
    sum_im = jnp.einsum("cta,tr->cra", prod_im, member, precision=lax.Precision.HIGHEST)
    return (sum_re, sum_im)


def per_device(y_start, tile_real, tile_imag, tile_rows, tile_slots, fetch_pick):
    group, rows = y_start.shape
    order = tile_real.shape[1]
    rb_dev = rows // order
    local_count = LOC_RB * rb_dev
    nblk = lax.axis_size("blk")
    member = (tile_rows[:, None] == jnp.arange(rb_dev, dtype=jnp.int32)[None, :]).astype(
        jnp.float32
    )
    present = jnp.abs(tile_real) + jnp.abs(tile_imag)
    counted = jnp.einsum(
        "tab,b->ta", present, jnp.ones((order,), jnp.bfloat16), preferred_element_type=jnp.float32
    )
    degree = jnp.dot(member.T, counted, precision=lax.Precision.HIGHEST)
    scale = (1.0 / jnp.sqrt(jnp.maximum(degree, 1.0))).reshape(rows)
    own_slots = tile_slots[:local_count]
    owners = tile_slots[local_count:] - rb_dev
    fetch_row = fetch_pick[0]
    real_near, imag_near, member_near = (
        tile_real[:local_count],
        tile_imag[:local_count],
        member[:local_count],
    )
    real_far, imag_far, member_far = (
        tile_real[local_count:],
        tile_imag[local_count:],
        member[local_count:],
    )
    wanted = lax.all_to_all(fetch_row, "blk", split_axis=0, concat_axis=0, tiled=True)

    def operate(field):
        sent = (field * scale[None, :]).astype(jnp.bfloat16).reshape(group, rb_dev, order)
        near = jnp.take(sent, own_slots, axis=1)
        near_re, near_im = tile_products(near, real_near, imag_near, member_near)
        packed = jnp.take(sent, wanted, axis=1)
        arrived = lax.all_to_all(packed, "blk", split_axis=1, concat_axis=1, tiled=True)
        far = jnp.take(arrived, owners, axis=1)
        far_re, far_im = tile_products(far, real_far, imag_far, member_far)
        applied = (near_re + far_re + turn(near_im + far_im)).reshape(group, rows) * scale[None, :]
        return ((1.0 - center) * field - applied) / half_width

    previous = y_start
    current = operate(y_start)
    for step in range(1, STEPS):
        following = 2.0 * operate(current) - previous
        previous, current = (current, following)
    gathered = lax.all_gather(current, "col", axis=0, tiled=True)
    partial_gram = jnp.dot(gathered, gathered.T, precision=lax.Precision.HIGHEST)
    gram = lax.psum(partial_gram, "blk")
    gram = gram + turn(turn(gram).T).T
    lower = jnp.linalg.cholesky(gram)
    solved = jax.scipy.linalg.solve_triangular(lower, gathered, lower=True)
    mine = lax.dynamic_slice_in_dim(solved, lax.axis_index("col") * group, group, 0)
    return mine * math.sqrt(rows * nblk)


def solution(mesh):
    return jax.shard_map(
        per_device,
        mesh=mesh,
        in_specs=(
            P("col", "blk"),
            P("blk", None, None),
            P("blk", None, None),
            P("blk"),
            P("blk"),
            P("blk", None),
        ),
        out_specs=P("col", "blk"),
        check_vma=False,
    )
```

profile of v0, /device:TPU:1, one launch (start us, length us, event | category | flops | bytes accessed | tf_op | source)
XLA Modules:
  0.0 487.0 jit_solution(1898330010088756384)
XLA Ops:
  7.9 13.2 %all-to-all-start = ((s32[64,1,1]{2,1,0:T(1,128)}), s32[64,1,1]{2,1,0:T(1,128)S(1)}, u32[]{:S(2)}, u32[]{:S(2)}) async-start(s32[64,1,1]{2,1,0:T(1,128)} %copy.73), calls=%async_computation | async-start | bytes 65536 | tf_op jit(solution)/shard_map/all_to_all | solution.py:57
  21.1 10.0 %fusion = f32[1,96,256]{2,0,1:T(1,128)S(1)} fusion(bf16[96,256,256]{2,1,0:T(8,128)(2,1)} %param.14, bf16[96,256,256]{2,1,0:T(8,128)(2,1)} %param.13), kind=kOutput, calls=%fused_computation.12 | convolution fusion | flops 31457280 | bytes 25264128 | tf_op jit(solution)/shard_map/tab,b->ta/dot_general | solution.py:39
  34.4 10.6 %all-to-all-start.1 = ((bf16[32,64,256]{2,0,1:T(8,128)(2,1)}), bf16[32,64,256]{2,0,1:T(8,128)(2,1)S(1)}, u32[]{:S(2)}, u32[]{:S(2)}) async-start(bf16[32,64,256]{2,0,1:T(8,128)(2,1)} %select_bitcast_fusion.3), calls=%async_computation.1 | async-start | bytes 2097152 | tf_op jit(solution)/shard_map/all_to_all | solution.py:64
  48.0 3.1 fusion.84
  51.2 21.7 %all-to-all-done.1 = bf16[32,64,256]{2,0,1:T(8,128)(2,1)S(1)} async-done(((bf16[32,64,256]{2,0,1:T(8,128)(2,1)}), bf16[32,64,256]{2,0,1:T(8,128)(2,1)S(1)}, u32[]{:S(2)}, u32[]{:S(2)}) %all-to-all-start.1) | async-done | bytes 1048608 | tf_op jit(solution)/shard_map/all_to_all | solution.py:64
  73.5 5.7 %fusion.48 = f32[32,80,256]{2,0,1:T(8,128)S(1)} fusion(bf16[96,256,256]{2,1,0:T(8,128)(2,1)} %param.14, bf16[80,32,256]{2,1,0:T(8,128)(2,1)S(1)} %gather_fusion.2, pred[80]{0:T(512)(128)(4,1)S(1)} %get-tuple-element.10), kind=kOutput, calls=%fused_computation.52 | convolution fusion | flops 336199680 | bytes 14418000 | tf_op jit(solution)/shard_map/ctb,tab->cta/dot_general | solution.py:23
  79.2 5.7 %fusion.36 = f32[32,80,256]{2,0,1:T(8,128)S(1)} fusion(bf16[96,256,256]{2,1,0:T(8,128)(2,1)} %param.13, bf16[80,32,256]{2,1,0:T(8,128)(2,1)S(1)} %gather_fusion.2, pred[80]{0:T(512)(128)(4,1)S(1)} %get-tuple-element.10), kind=kOutput, calls=%fused_computation.48 | convolution fusion | flops 336199680 | bytes 14418000 | tf_op jit(solution)/shard_map/ctb,tab->cta/dot_general | solution.py:22
  85.0 2.4 fusion.32
  88.1 2.4 fusion.34
  93.1 6.8 %all-to-all-start.2 = ((bf16[32,64,256]{2,0,1:T(8,128)(2,1)}), bf16[32,64,256]{2,0,1:T(8,128)(2,1)S(1)}, u32[]{:S(2)}, u32[]{:S(2)}) async-start(bf16[32,64,256]{2,0,1:T(8,128)(2,1)} %select_bitcast_fusion.2), calls=%async_computation.2 | async-start | bytes 2097152 | tf_op jit(solution)/shard_map/all_to_all | solution.py:64
  102.8 3.1 fusion.87
  105.9 21.8 %all-to-all-done.2 = bf16[32,64,256]{2,0,1:T(8,128)(2,1)S(1)} async-done(((bf16[32,64,256]{2,0,1:T(8,128)(2,1)}), bf16[32,64,256]{2,0,1:T(8,128)(2,1)S(1)}, u32[]{:S(2)}, u32[]{:S(2)}) %all-to-all-start.2) | async-done | bytes 1048608 | tf_op jit(solution)/shard_map/all_to_all | solution.py:64
  128.6 5.7 %fusion.51 = f32[32,80,256]{2,0,1:T(8,128)S(1)} fusion(bf16[96,256,256]{2,1,0:T(8,128)(2,1)} %param.14, bf16[80,32,256]{2,1,0:T(8,128)(2,1)S(1)} %gather_fusion.5, pred[80]{0:T(512)(128)(4,1)S(1)} %get-tuple-element.10), kind=kOutput, calls=%fused_computation.53 | convolution fusion | flops 336199680 | bytes 14418000 | tf_op jit(solution)/shard_map/ctb,tab->cta/dot_general | solution.py:23
  134.3 5.7 %fusion.39 = f32[32,80,256]{2,0,1:T(8,128)S(1)} fusion(bf16[96,256,256]{2,1,0:T(8,128)(2,1)} %param.13, bf16[80,32,256]{2,1,0:T(8,128)(2,1)S(1)} %gather_fusion.5, pred[80]{0:T(512)(128)(4,1)S(1)} %get-tuple-element.10), kind=kOutput, calls=%fused_computation.49 | convolution fusion | flops 336199680 | bytes 14418000 | tf_op jit(solution)/shard_map/ctb,tab->cta/dot_general | solution.py:22
  143.1 2.4 fusion.30
  148.3 7.0 %all-to-all-start.3 = ((bf16[32,64,256]{2,0,1:T(8,128)(2,1)}), bf16[32,64,256]{2,0,1:T(8,128)(2,1)S(1)}, u32[]{:S(2)}, u32[]{:S(2)}) async-start(bf16[32,64,256]{2,0,1:T(8,128)(2,1)} %select_bitcast_fusion.1), calls=%async_computation.3 | async-start | bytes 2097152 | tf_op jit(solution)/shard_map/all_to_all | solution.py:64
  156.0 3.1 fusion.102
  159.1 3.1 fusion.90
  162.2 20.9 %all-to-all-done.3 = bf16[32,64,256]{2,0,1:T(8,128)(2,1)S(1)} async-done(((bf16[32,64,256]{2,0,1:T(8,128)(2,1)}), bf16[32,64,256]{2,0,1:T(8,128)(2,1)S(1)}, u32[]{:S(2)}, u32[]{:S(2)}) %all-to-all-start.3) | async-done | bytes 1048608 | tf_op jit(solution)/shard_map/all_to_all | solution.py:64
  183.9 5.7 %fusion.54 = f32[32,80,256]{2,0,1:T(8,128)S(1)} fusion(bf16[96,256,256]{2,1,0:T(8,128)(2,1)} %param.14, bf16[80,32,256]{2,1,0:T(8,128)(2,1)S(1)} %gather_fusion.8, pred[80]{0:T(512)(128)(4,1)S(1)} %get-tuple-element.10), kind=kOutput, calls=%fused_computation.54 | convolution fusion | flops 336199680 | bytes 14418000 | tf_op jit(solution)/shard_map/ctb,tab->cta/dot_general | solution.py:23
  189.7 5.7 %fusion.42 = f32[32,80,256]{2,0,1:T(8,128)S(1)} fusion(bf16[96,256,256]{2,1,0:T(8,128)(2,1)} %param.13, bf16[80,32,256]{2,1,0:T(8,128)(2,1)S(1)} %gather_fusion.8, pred[80]{0:T(512)(128)(4,1)S(1)} %get-tuple-element.10), kind=kOutput, calls=%fused_computation.50 | convolution fusion | flops 336199680 | bytes 14418000 | tf_op jit(solution)/shard_map/ctb,tab->cta/dot_general | solution.py:22
  203.7 6.5 %all-to-all-start.4 = ((bf16[32,64,256]{2,0,1:T(8,128)(2,1)}), bf16[32,64,256]{2,0,1:T(8,128)(2,1)S(1)}, u32[]{:S(2)}, u32[]{:S(2)}) async-start(bf16[32,64,256]{2,0,1:T(8,128)(2,1)} %select_bitcast_fusion), calls=%async_computation.4 | async-start | bytes 2097152 | tf_op jit(solution)/shard_map/all_to_all | solution.py:64
  211.1 3.1 fusion.105
  214.3 3.1 fusion.93
  217.4 20.8 %all-to-all-done.4 = bf16[32,64,256]{2,0,1:T(8,128)(2,1)S(1)} async-done(((bf16[32,64,256]{2,0,1:T(8,128)(2,1)}), bf16[32,64,256]{2,0,1:T(8,128)(2,1)S(1)}, u32[]{:S(2)}, u32[]{:S(2)}) %all-to-all-start.4) | async-done | bytes 1048608 | tf_op jit(solution)/shard_map/all_to_all | solution.py:64
  239.0 5.7 %fusion.57 = f32[32,80,256]{2,0,1:T(8,128)S(1)} fusion(bf16[96,256,256]{2,1,0:T(8,128)(2,1)} %param.14, bf16[80,32,256]{2,1,0:T(8,128)(2,1)S(1)} %gather_fusion.11, pred[80]{0:T(512)(128)(4,1)S(1)} %get-tuple-element.10), kind=kOutput, calls=%fused_computation.55 | convolution fusion | flops 336199680 | bytes 14418000 | tf_op jit(solution)/shard_map/ctb,tab->cta/dot_general | solution.py:23
  244.7 5.7 %fusion.45 = f32[32,80,256]{2,0,1:T(8,128)S(1)} fusion(bf16[96,256,256]{2,1,0:T(8,128)(2,1)} %param.13, bf16[80,32,256]{2,1,0:T(8,128)(2,1)S(1)} %gather_fusion.11, pred[80]{0:T(512)(128)(4,1)S(1)} %get-tuple-element.10), kind=kOutput, calls=%fused_computation.51 | convolution fusion | flops 336199680 | bytes 14418000 | tf_op jit(solution)/shard_map/ctb,tab->cta/dot_general | solution.py:22
  257.9 22.6 %all-gather.2.cloned.1.call-done = f32[128,2048]{1,0:T(8,128)} async-done(((f32[32,2048]{1,0:T(8,128)}), f32[128,2048]{1,0:T(8,128)}) %all-gather.2.cloned.1.call-update) | async-done | bytes 1048592 | tf_op jit(solution)/shard_map/all_gather | solution.py:75
  280.5 3.3 fusion.190
  283.8 169.2 %all-reduce.2.cloned.1.call-done = f32[128,128]{0,1:T(8,128)} async-done(((f32[128,128]{0,1:T(8,128)}), f32[128,128]{0,1:T(8,128)}) %all-reduce.2.cloned.1.call-update) | async-done | bytes 65552 | tf_op jit(solution)/shard_map/psum | solution.py:77
  455.3 11.7 %cholesky.16 = f32[128,128]{1,0:T(8,128)S(1)} custom-call(f32[128,128]{1,0:T(8,128)S(1)} %fusion.139), custom_call_target="Cholesky" | custom-call | tf_op jit(solution)/shard_map/jit(cholesky)/cholesky | solution.py:79
  468.3 9.8 %custom-call.7 = f32[1,128,128]{1,2,0:T(8,128)S(1)} custom-call(f32[1,128,128]{2,1,0:T(8,128)S(1)} %fusion.136), custom_call_target="InvertDiagBlocksLowerTriangular" | custom-call | tf_op jit(solution)/shard_map/jit(_solve_triangular)/triangular_solve | solution.py:80
  (124 shorter events, 44.9 us)
Async XLA Ops:
  7.9 23.4 %all-to-all-start = ((s32[64,1,1]{2,1,0:T(1,128)}), s32[64,1,1]{2,1,0:T(1,128)S(1)}, u32[]{:S(2)}, u32[]{:S(2)}) async-start(s32[64,1,1]{2,1,0:T(1,128)} %copy.73), calls=%async_computation | async-start | bytes 65536 | tf_op jit(solution)/shard_map/all_to_all | solution.py:57
  21.1 10.0 %copy-start.18 = (s32[96]{0:T(128)S(1)}, s32[96]{0:T(128)}, u32[]{:S(2)}) copy-start(s32[96]{0:T(128)} %param.15) | copy-start | bytes 1156
  21.1 10.2 %copy-start.1 = (f32[32,2048]{1,0:T(8,128)S(1)}, f32[32,2048]{1,0:T(8,128)}, u32[]{:S(2)}) copy-start(f32[32,2048]{1,0:T(8,128)} %param.12) | copy-start | bytes 786436
  32.6 59.4 %copy-start.15 = (pred[64]{0:T(512)(128)(4,1)}, pred[64]{0:T(512)(128)(4,1)S(1)}, u32[]{:S(2)}) copy-start(pred[64]{0:T(512)(128)(4,1)S(1)} %compare_and_fusion.1) | copy-start | bytes 196
  32.6 58.7 %copy-start.12 = (s32[1024]{0:T(1024)}, s32[1024]{0:T(1024)S(1)}, u32[]{:S(2)}) copy-start(s32[1024]{0:T(1024)S(1)} %pad_clamp_fusion.1) | copy-start | bytes 12292
  33.2 11.7 %copy-start.19 = (s32[96]{0:T(128)S(1)}, s32[96]{0:T(128)}, u32[]{:S(2)}) copy-start(s32[96]{0:T(128)} %param.16) | copy-start | bytes 1156
  34.4 38.4 %all-to-all-start.1 = ((bf16[32,64,256]{2,0,1:T(8,128)(2,1)}), bf16[32,64,256]{2,0,1:T(8,128)(2,1)S(1)}, u32[]{:S(2)}, u32[]{:S(2)}) async-start(bf16[32,64,256]{2,0,1:T(8,128)(2,1)} %select_bitcast_fusion.3), calls=%async_computation.1 | async-start | bytes 2097152 | tf_op jit(solution)/shard_map/all_to_all | solution.py:64
  45.0 6.2 %copy-start.8 = (pred[16]{0:T(512)(128)(4,1)}, pred[16]{0:T(512)(128)(4,1)S(1)}, u32[]{:S(2)}) copy-start(pred[16]{0:T(512)(128)(4,1)S(1)} %get-tuple-element.6) | copy-start | bytes 52
  45.0 54.9 %copy-start.13 = (s32[1024]{0:T(1024)}, s32[1024]{0:T(1024)S(1)}, u32[]{:S(2)}) copy-start(s32[1024]{0:T(1024)S(1)} %pad_clamp_fusion.2) | copy-start | bytes 12292
  45.7 27.1 %copy-start.14 = (s32[1024]{0:T(1024)}, s32[1024]{0:T(1024)S(1)}, u32[]{:S(2)}) copy-start(s32[1024]{0:T(1024)S(1)} %pad_clamp_fusion) | copy-start | bytes 12292
  87.4 3.1 copy-start.5
  91.9 8.5 %copy-start.9 = (pred[16]{0:T(512)(128)(4,1)S(1)}, pred[16]{0:T(512)(128)(4,1)}, u32[]{:S(2)}) copy-start(pred[16]{0:T(512)(128)(4,1)} %copy-done.8) | copy-start | bytes 52
  93.1 34.7 %all-to-all-start.2 = ((bf16[32,64,256]{2,0,1:T(8,128)(2,1)}), bf16[32,64,256]{2,0,1:T(8,128)(2,1)S(1)}, u32[]{:S(2)}, u32[]{:S(2)}) async-start(bf16[32,64,256]{2,0,1:T(8,128)(2,1)} %select_bitcast_fusion.2), calls=%async_computation.2 | async-start | bytes 2097152 | tf_op jit(solution)/shard_map/all_to_all | solution.py:64
  142.4 3.1 copy-start.6
  145.5 1.6 copy-start.16
  147.1 8.8 %copy-start.10 = (pred[16]{0:T(512)(128)(4,1)S(1)}, pred[16]{0:T(512)(128)(4,1)}, u32[]{:S(2)}) copy-start(pred[16]{0:T(512)(128)(4,1)} %copy-done.8) | copy-start | bytes 52
  148.3 34.8 %all-to-all-start.3 = ((bf16[32,64,256]{2,0,1:T(8,128)(2,1)}), bf16[32,64,256]{2,0,1:T(8,128)(2,1)S(1)}, u32[]{:S(2)}, u32[]{:S(2)}) async-start(bf16[32,64,256]{2,0,1:T(8,128)(2,1)} %select_bitcast_fusion.1), calls=%async_computation.3 | async-start | bytes 2097152 | tf_op jit(solution)/shard_map/all_to_all | solution.py:64
  195.4 2.4 copy-start.3
  197.8 3.1 copy-start.7
  200.9 1.6 copy-start.17
  202.6 8.5 %copy-start.11 = (pred[16]{0:T(512)(128)(4,1)S(1)}, pred[16]{0:T(512)(128)(4,1)}, u32[]{:S(2)}) copy-start(pred[16]{0:T(512)(128)(4,1)} %copy-done.8) | copy-start | bytes 52
  203.7 34.5 %all-to-all-start.4 = ((bf16[32,64,256]{2,0,1:T(8,128)(2,1)}), bf16[32,64,256]{2,0,1:T(8,128)(2,1)S(1)}, u32[]{:S(2)}, u32[]{:S(2)}) async-start(bf16[32,64,256]{2,0,1:T(8,128)(2,1)} %select_bitcast_fusion), calls=%async_computation.4 | async-start | bytes 2097152 | tf_op jit(solution)/shard_map/all_to_all | solution.py:64
  210.2 70.3 %all-gather.2.cloned.1.call-start = ((), (), s32[]{:S(2)}) async-start(), calls=%async_computation.5 | async-start | bytes 1310720 | tf_op jit(solution)/shard_map/all_gather | solution.py:75
  250.5 2.4 copy-start.2
  252.9 3.1 copy-start.4
  257.6 195.4 %all-reduce.2.cloned.1.call-start = ((), (), s32[]{:S(2)}) async-start(), calls=%async_computation.6 | async-start | bytes 131072 | tf_op jit(solution)/shard_map/psum | solution.py:77
  280.5 197.7 %copy-start = (f32[128,2048]{1,0:T(8,128)S(1)}, f32[128,2048]{1,0:T(8,128)}, u32[]{:S(2)}) copy-start(f32[128,2048]{1,0:T(8,128)} %all-gather.2.cloned.1.call-done) | copy-start | bytes 3145732
Sparse Core Ops, SparseCore 0:
  257.7 22.6 all-gather.1
  283.9 169.0 all-reduce.1
where the time goes:
time: 492 us; the launch traced here: 487 us
  waiting for transfers between devices  277 us (56%)
  matrix products  108 us (22%)
  starting transfers between devices  44.4 us (9%)
  other arithmetic  31.9 us (6%)
  between operations  14.5 us (3%)
  local copies, waits for them, and re-layouts  11.2 us (2%)
    psum x1, waiting for transfers between devices, per_device(): gram = lax.psum(partial_gram, 'blk')  169 us
    all_to_all x4, waiting for transfers between devices, operate(): lax.all_to_all(packed, 'blk', split_axis=1, concat_axis=1, tiled=True)  85.2 us
    dot_general x8, matrix products, tile_products(): jnp.einsum('ctb,tab->cta', picked, real_part, preferred_element_type=jnp....  35.4 us
    dot_general x8, matrix products, tile_products(): jnp.einsum('ctb,tab->cta', picked, imag_part, preferred_element_type=jnp....  33.7 us
    all_to_all x4, starting transfers between devices, operate(): lax.all_to_all(packed, 'blk', split_axis=1, concat_axis=1, tiled=True)  30.8 us
    all_gather x1, waiting for transfers between devices, per_device(): gathered = lax.all_gather(current, 'col', axis=0, tiled=True)  22.6 us
    all_to_all x1, starting transfers between devices, per_device(): lax.all_to_all(fetch_row, 'blk', split_axis=0, concat_axis=0, tiled=True)  13.2 us
    another operation x3, other arithmetic, per_device(): lower = jnp.linalg.cholesky(gram)  12.4 us
  transfers between devices with their start and end apart: 7, of which 6 were waited for; matrix products, arithmetic and copies ran while one was open for 7% of the time, Pallas kernels for 0%

commit v1 on v0

v1 whole, which is shorter than its diff:
```python
import math

import jax
import jax.numpy as jnp
from jax import lax
from jax.experimental import pallas as pl
from jax.experimental.pallas import tpu as pltpu
from jax.sharding import PartitionSpec as P

STEPS = 4
NEAR = 16
TILES = 96
RB = 8
GROUP = 32
HALF = 16
ORDER = 256
NZ, NY = 8, 4
CHUNK = 8
UNROLL = 16
MESH = pl.DeviceIdType.MESH

center = 1.25
half_width = 0.75

Z_PLACE = (0, 2, 4, 6, 7, 5, 3, 1)
Z_OFFSET = (0, 7, 1, 6, 2, 5, 3, 4)
GROUPS = ((0, 1), (1, 2), (3, 2), (5, 2), (7, 1))


def turn(values):
    pairs = values.reshape((values.shape[0] // 2, 2) + values.shape[1:])
    return jnp.stack([-pairs[:, 1], pairs[:, 0]], axis=1).reshape(values.shape)


def filter_kernel(
    prev_ref, last_ref, src_ref, y_ref, picks_ref, real_ref, imag_ref, out_ref, *scratch
):
    own = scratch[0:2]
    zbuf = (None,) + tuple(scratch[2 + 2 * i : 4 + 2 * i] for i in range(7))
    arr = scratch[16:18]
    stage = scratch[18:20]
    (
        weights, raw, sums, degs, scale, field, before,
        pick_in, pick_s,
        raw_sem, pick_send, pick_recv, pick_loc, z_send, z_recv, y_send, y_recv,
    ) = scratch[20:]
    me = lax.axis_index("blk")
    zi, yi, ci = me // 8, (me // 2) % NY, me % 2
    up = ((zi + 1) % NZ) * 8 + yi * 2 + ci
    down = ((zi + NZ - 1) % NZ) * 8 + yi * 2 + ci

    def partner(j):
        dy, dc = j // 2, j % 2
        return zi * 8 + ((yi + dy) % NY) * 2 + (ci + dc) % 2

    barrier = pltpu.get_barrier_semaphore()
    for other in [up, down] + [partner(j) for j in range(1, 8)]:
        pl.semaphore_signal(barrier, inc=1, device_id={"blk": other}, device_id_type=MESH)

    def raw_copies(k):
        return [
            pltpu.make_async_copy(
                ref.at[pl.ds(k * CHUNK, CHUNK)], raw.at[k % 2, i], raw_sem.at[k % 2, i]
            )
            for i, ref in enumerate((real_ref, imag_ref))
        ]

    for copy in raw_copies(0):
        copy.start()
    pl.semaphore_wait(barrier, 9)

    def pick_copy(j):
        return pltpu.make_async_remote_copy(
            src_ref=picks_ref,
            dst_ref=pick_in.at[j],
            send_sem=pick_send.at[j],
            recv_sem=pick_recv.at[j],
            device_id={"blk": partner(j)},
            device_id_type=MESH,
        )

    for j in range(1, 8):
        pick_copy(j).start()

    degs[0] = jnp.zeros((8, ORDER), jnp.float32)
    sums[0] = jnp.zeros((GROUP, ORDER), jnp.float32)
    ones = jnp.ones((8, ORDER), jnp.bfloat16)

    def load_chunk(k, carry):
        @pl.when(k + 1 < TILES // CHUNK)
        def _():
            for copy in raw_copies(k + 1):
                copy.start()

        for copy in raw_copies(k):
            copy.wait()

        def one(i, c):
            t = k * CHUNK + i
            re_t = raw[k % 2, 0, i].T
            im_t = raw[k % 2, 1, i].T
            weights[t, 0:ORDER] = re_t
            weights[t, ORDER : 2 * ORDER] = im_t
            count = jnp.dot(ones, jnp.abs(re_t) + jnp.abs(im_t), preferred_element_type=jnp.float32)
            degs[t + 1] = count + degs[prev_ref[t]]
            return c

        return lax.fori_loop(0, CHUNK, one, carry, unroll=4)

    lax.fori_loop(0, TILES // CHUNK, load_chunk, 0)
    for r in range(RB):
        scale[r] = 1.0 / jnp.sqrt(jnp.maximum(degs[last_ref[r]], 1.0))

    pick_in[0] = picks_ref[...]
    for j in range(1, 8):
        pick_copy(j).wait()
    to_smem = pltpu.make_async_copy(pick_in, pick_s, pick_loc.at[0])
    to_smem.start()
    to_smem.wait()

    field[...] = y_ref[...]

    def z_copy(par, way, hop, half):
        place_in = 2 * hop - 1 + way if hop > 0 else 0
        place_out = 2 * hop + 1 + way if hop < 3 else 7
        source = own[par] if hop == 0 else zbuf[place_in][par]
        part = pl.ds(half * 4, 4)
        return pltpu.make_async_remote_copy(
            src_ref=source.at[part],
            dst_ref=zbuf[place_out][par].at[part],
            send_sem=z_send.at[par, way, hop, half],
            recv_sem=z_recv.at[par, way, hop, half],
            device_id={"blk": down if way else up},
            device_id_type=MESH,
        )

    def y_copy(par, j, g):
        first, count = GROUPS[g]
        return pltpu.make_async_remote_copy(
            src_ref=stage[par].at[j, pl.ds(first, count)],
            dst_ref=arr[par].at[j, pl.ds(first, count)],
            send_sem=y_send.at[par, j, g],
            recv_sem=y_recv.at[par, j, g],
            device_id={"blk": partner(j)},
            device_id_type=MESH,
        )

    def hand_on(par, g):
        first, count = GROUPS[g]
        for j in (2, 3, 6, 7, 4, 5, 1, 0):
            if j == 0 and g == 0:
                continue
            for k in range(first, first + count):
                source = own[par] if k == 0 else zbuf[k][par]
                owner = ((zi + Z_OFFSET[k]) % NZ) * 8 + yi * 2 + ci
                row = ((4 - j // 2) % 4) * 2 + j % 2
                block = source[pick_s[row, 0, owner]]
                if j == 0:
                    arr[par][0, k] = block
                else:
                    stage[par][j, k] = block
            if j != 0:
                y_copy(par, j, g).start()

    def product(block, t):
        lower = block[HALF:GROUP]
        left = jnp.concatenate([block, jnp.concatenate([-lower, block[0:HALF]], axis=0)], axis=1)
        sums[t + 1] = sums[prev_ref[t]] + jnp.dot(
            left, weights[t], preferred_element_type=jnp.float32
        )

    for step in range(STEPS):
        par = step % 2
        for r in range(RB):
            s4 = jnp.concatenate([scale[r]] * 4, axis=0)
            own[par][r] = (field[r] * s4).astype(jnp.bfloat16)
        for half in range(2):
            for way in range(2):
                z_copy(par, way, 0, half).start()
        hand_on(par, 0)

        def near(t, c):
            product(own[par][src_ref[t]], t)
            return c

        lax.fori_loop(0, NEAR, near, 0, unroll=UNROLL)
        for hop in range(1, 4):
            for half in range(2):
                for way in range(2):
                    z_copy(par, way, hop - 1, half).wait_recv()
                    if hop < 3 or half == way:
                        z_copy(par, way, hop, half).start()
            hand_on(par, hop)
        for way in range(2):
            z_copy(par, way, 3, way).wait_recv()
        hand_on(par, 4)
        for g in range(5):
            for j in range(1, 8):
                y_copy(par, j, g).wait_recv()

        def far(t, c):
            place = src_ref[t]
            product(arr[par][place // 8, place % 8], t)
            return c

        lax.fori_loop(NEAR, TILES, far, 0, unroll=UNROLL)
        for r in range(RB):
            s4 = jnp.concatenate([scale[r]] * 4, axis=0)
            now = field[r]
            moved = ((1.0 - center) * now - sums[last_ref[r]] * s4) / half_width
            if step > 0:
                moved = 2.0 * moved - before[r]
            if step < STEPS - 1:
                before[r] = now
                field[r] = moved
            else:
                out_ref[r] = moved
        for hop in range(4):
            for way in range(2):
                for half in range(2):
                    if hop < 3 or half == way:
                        z_copy(par, way, hop, half).wait_send()
        for g in range(5):
            for j in range(1, 8):
                y_copy(par, j, g).wait_send()


def chebyshev(y_start, tile_real, tile_imag, tile_rows, tile_slots, fetch_pick):
    me = lax.axis_index("blk")
    zi, yi, ci = me // 8, (me // 2) % NY, me % 2
    order = jnp.arange(TILES, dtype=jnp.int32)
    same = (tile_rows[:, None] == tile_rows[None, :]) & (order[None, :] < order[:, None])
    prev = jnp.max(jnp.where(same, order[None, :] + 1, 0), axis=1)
    here = tile_rows[None, :] == jnp.arange(RB, dtype=jnp.int32)[:, None]
    last = jnp.max(jnp.where(here, order[None, :] + 1, 0), axis=1)
    owner = tile_slots - RB
    zp, yp, cp = owner // 8, (owner // 2) % NY, owner % 2
    dz = (zp - zi) % NZ
    place = jnp.where(
        dz == 0, 0, jnp.where(dz < 4, 2 * dz, jnp.where(dz == 4, 7, 2 * (8 - dz) - 1))
    )
    j = ((yi - yp) % NY) * 2 + (ci + cp) % 2
    src = jnp.where(order < NEAR, tile_slots, j * 8 + place)
    picks = jnp.pad(fetch_pick, ((0, 7), (0, 64)))
    block = (RB, GROUP, ORDER)
    split = y_start.reshape(HALF, 2, RB, ORDER).transpose(2, 1, 0, 3).reshape(block)
    done = pl.pallas_call(
        filter_kernel,
        name="filter",
        out_shape=jax.ShapeDtypeStruct(block, jnp.float32),
        in_specs=[pl.BlockSpec(memory_space=pltpu.SMEM)] * 3
        + [pl.BlockSpec(memory_space=pltpu.VMEM)] * 2
        + [pl.BlockSpec(memory_space=pl.ANY)] * 2,
        out_specs=pl.BlockSpec(memory_space=pltpu.VMEM),
        scratch_shapes=[pltpu.VMEM(block, jnp.bfloat16)] * 16
        + [pltpu.VMEM((8,) + block, jnp.bfloat16)] * 4
        + [
            pltpu.VMEM((TILES, 2 * ORDER, ORDER), jnp.bfloat16),
            pltpu.VMEM((2, 2, CHUNK, ORDER, ORDER), jnp.bfloat16),
            pltpu.VMEM((TILES + 1, GROUP, ORDER), jnp.float32),
            pltpu.VMEM((TILES + 1, 8, ORDER), jnp.float32),
            pltpu.VMEM((RB, 8, ORDER), jnp.float32),
            pltpu.VMEM(block, jnp.float32),
            pltpu.VMEM(block, jnp.float32),
            pltpu.VMEM((8, 8, 128), jnp.int32),
            pltpu.SMEM((8, 8, 128), jnp.int32),
            pltpu.SemaphoreType.DMA((2, 2)),
            pltpu.SemaphoreType.DMA((8,)),
            pltpu.SemaphoreType.DMA((8,)),
            pltpu.SemaphoreType.DMA((1,)),
            pltpu.SemaphoreType.DMA((2, 2, 4, 2)),
            pltpu.SemaphoreType.DMA((2, 2, 4, 2)),
            pltpu.SemaphoreType.DMA((2, 8, 5)),
            pltpu.SemaphoreType.DMA((2, 8, 5)),
        ],
        compiler_params=pltpu.CompilerParams(
            collective_id=0, has_side_effects=True, vmem_limit_bytes=58 << 20
        ),
    )(prev, last, src, split, picks, tile_real, tile_imag)
    return done.reshape(RB, 2, HALF, ORDER).transpose(2, 1, 0, 3).reshape(y_start.shape)


def per_device(y_start, tile_real, tile_imag, tile_rows, tile_slots, fetch_pick):
    group, rows = y_start.shape
    nblk = lax.axis_size("blk")
    current = chebyshev(y_start, tile_real, tile_imag, tile_rows, tile_slots, fetch_pick)
    gathered = lax.all_gather(current, "col", axis=0, tiled=True)
    partial_gram = jnp.dot(gathered, gathered.T, precision=lax.Precision.HIGHEST)
    gram = lax.psum(partial_gram, "blk")
    gram = gram + turn(turn(gram).T).T
    lower = jnp.linalg.cholesky(gram)
    solved = jax.scipy.linalg.solve_triangular(lower, gathered, lower=True)
    mine = lax.dynamic_slice_in_dim(solved, lax.axis_index("col") * group, group, 0)
    return mine * math.sqrt(rows * nblk)


def solution(mesh):
    return jax.shard_map(
        per_device,
        mesh=mesh,
        in_specs=(
            P("col", "blk"),
            P("blk", None, None),
            P("blk", None, None),
            P("blk"),
            P("blk"),
            P("blk", None),
        ),
        out_specs=P("col", "blk"),
        check_vma=False,
    )
```

time: 492 us -> 375 us (0.76)
  Pallas kernels: 0 us -> 129 us
  matrix products: 108 us -> 5.43 us
  waiting for transfers between devices: 277 us -> 192 us
  starting transfers between devices: 44.4 us -> 0.22 us
  local copies, waits for them, and re-layouts: 11.2 us -> 6.14 us
    pallas_call x0 -> x1, Pallas kernels: none -> 129 us  [chebyshev(): pl.pallas_call(filter_kernel, name='filter', out_shape=jax.ShapeDtypeStru...]
    dot_general x34 -> x0, matrix products: 104 us -> none  [the longest x8 35.4 us: tile_products(): jnp.einsum('ctb,tab->cta', picked, real_part, preferred_element_type=jnp....]
    all_to_all x5 -> x0, waiting for transfers between devices: 85.2 us -> none  [the longest x4 85.2 us: operate(): lax.all_to_all(packed, 'blk', split_axis=1, concat_axis=1, tiled=True)]
    all_to_all x5 -> x0, starting transfers between devices: 44 us -> none  [the longest x4 30.8 us: operate(): lax.all_to_all(packed, 'blk', split_axis=1, concat_axis=1, tiled=True)]
    gather x12 -> x0, local copies, waits for them, and re-layouts: 8.27 us -> none  [the longest x4 3.08 us: operate(): far = jnp.take(arrived, owners, axis=1)]
  transfers between devices with their start and end apart: 7 -> 2, of which waited for: 6 -> 2; matrix products, arithmetic and copies ran while one was open for 7% -> 0% of each run, Pallas kernels for 0% -> 0%
where the time goes in v1:
time: 375 us
  waiting for transfers between devices  192 us (51%)
  Pallas kernels  129 us (34%)
  other arithmetic  28.7 us (8%)
  between operations  13.5 us (4%)
  local copies, waits for them, and re-layouts  6.14 us (2%)
  matrix products  5.43 us (1%)
    psum x1, waiting for transfers between devices, per_device(): gram = lax.psum(partial_gram, 'blk')  169 us
    pallas_call x1, Pallas kernels, chebyshev(): pl.pallas_call(filter_kernel, name='filter', out_shape=jax.ShapeDtypeStru...  129 us
    all_gather x1, waiting for transfers between devices, per_device(): gathered = lax.all_gather(current, 'col', axis=0, tiled=True)  22.7 us
    another operation x3, other arithmetic, per_device(): lower = jnp.linalg.cholesky(gram)  12.4 us
    another operation x2, other arithmetic, per_device(): solved = jax.scipy.linalg.solve_triangular(lower, gathered, lower=True)  10.5 us
  transfers between devices with their start and end apart: 2, of which 2 were waited for; matrix products, arithmetic and copies ran while one was open for 0% of the time, Pallas kernels for 0%

profile of v1, /device:TPU:1, one launch (start us, length us, event | category | flops | bytes accessed | tf_op | source)
XLA Modules:
  0.0 374.6 jit_solution(4484031876957689698)
XLA Ops:
  6.5 0.0 all-gather.2.cloned.1.call-start
  6.5 1.3 select_reduce_fusion.2.last_ref
  7.8 1.5 select_reduce_fusion.1.prev_ref
  9.2 1.2 pad.4.picks_ref
  10.5 1.0 copy.30
  11.5 0.9 copy.23
  12.4 1.3 compare_select_fusion.11.src_ref
  13.7 128.6 %filter.1 = f32[8,32,256]{2,1,0:T(8,128)} custom-call(s32[96]{0:T(128)} %select_reduce_fusion.1.prev_ref, s32[8]{0:T(128)} %select_reduce_fusion.2.last_ref, s32[96]{0:T(128)} %compare_select_fusion.11.src_ref, f32[8,32,256]{2,1,0:T(8,128)} %bitcast.31, s32[8,128]{1,0:T(8,128)} %pad.4.picks_ref, bf16[96,256,256]{2,1,0:T(8,128)(2,1)} %real_ref.1, ...), custom_call_target="tpu_custom_call" | custom-call | tf_op jit(solution)/shard_map/filter/pallas_call | solution.py:247
  142.2 1.1 copy.24
  143.3 0.8 copy.31
  144.1 0.0 all-gather.2.cloned.1.call-update
  144.2 0.2 all-reduce.3.cloned.1.call-start
  144.4 22.7 %all-gather.2.cloned.1.call-done = f32[128,2048]{1,0:T(8,128)} async-done(((f32[32,2048]{1,0:T(8,128)}), f32[128,2048]{1,0:T(8,128)}) %all-gather.2.cloned.1.call-update) | async-done | bytes 1048592 | tf_op jit(solution)/shard_map/all_gather | solution.py:287
  167.1 3.2 fusion.14
  170.3 0.0 all-reduce.3.cloned.1.call-update
  170.3 169.3 %all-reduce.3.cloned.1.call-done = f32[128,128]{0,1:T(8,128)} async-done(((f32[128,128]{0,1:T(8,128)}), f32[128,128]{0,1:T(8,128)}) %all-reduce.3.cloned.1.call-update) | async-done | bytes 65552 | tf_op jit(solution)/shard_map/psum | solution.py:289
  339.7 0.9 copy.26
  340.6 0.1 slice_negate_fusion.1
  340.7 0.1 pad_maximum_fusion
  340.7 0.1 copy.27
  340.8 0.1 slice_negate_fusion
  340.9 0.1 pad_maximum_fusion.1
  341.0 0.9 add.92
  341.8 0.1 copy.28
  341.9 11.7 %cholesky.16 = f32[128,128]{1,0:T(8,128)S(1)} custom-call(f32[128,128]{1,0:T(8,128)S(1)} %fusion.3), custom_call_target="Cholesky" | custom-call | tf_op jit(solution)/shard_map/jit(cholesky)/cholesky | solution.py:291
  353.7 0.6 compare_reduce_fusion
  354.3 0.7 fusion
  355.0 9.8 %custom-call.7 = f32[1,128,128]{1,2,0:T(8,128)S(1)} custom-call(f32[1,128,128]{2,1,0:T(8,128)S(1)} %fusion), custom_call_target="InvertDiagBlocksLowerTriangular" | custom-call | tf_op jit(solution)/shard_map/jit(_solve_triangular)/triangular_solve | solution.py:292
  364.8 2.3 fusion.1
  367.1 0.7 dynamic-slice_multiply_fusion
  (3 shorter events, 0.1 us)
Async XLA Ops:
  6.5 160.6 %all-gather.2.cloned.1.call-start = ((), (), s32[]{:S(2)}) async-start(), calls=%async_computation | async-start | bytes 1310720 | tf_op jit(solution)/shard_map/all_gather | solution.py:287
  144.2 195.5 %all-reduce.3.cloned.1.call-start = ((), (), s32[]{:S(2)}) async-start(), calls=%async_computation.1 | async-start | bytes 131072 | tf_op jit(solution)/shard_map/psum | solution.py:289
Sparse Core Ops, SparseCore 0:
  144.3 22.8 all-gather.1
  170.6 169.0 all-reduce.2

commit v2 on v1

--- a/solution.py
+++ b/solution.py
@@ -14,7 +14,10 @@
 GROUP = 32
 HALF = 16
 ORDER = 256
-NZ, NY = 8, 4
+NZ, NY, NX = 8, 4, 4
+PLANE = 32
+VEC = 64
+NODES = 131072
 CHUNK = 8
 UNROLL = 16
 MESH = pl.DeviceIdType.MESH
@@ -27,23 +30,19 @@
 GROUPS = ((0, 1), (1, 2), (3, 2), (5, 2), (7, 1))
 
 
-def turn(values):
-    pairs = values.reshape((values.shape[0] // 2, 2) + values.shape[1:])
-    return jnp.stack([-pairs[:, 1], pairs[:, 0]], axis=1).reshape(values.shape)
-
-
-def filter_kernel(
-    prev_ref, last_ref, src_ref, y_ref, picks_ref, real_ref, imag_ref, out_ref, *scratch
-):
+def filter_kernel(rows_ref, slots_ref, y_ref, picks_ref, real_ref, imag_ref, out_ref, *scratch):
     own = scratch[0:2]
     zbuf = (None,) + tuple(scratch[2 + 2 * i : 4 + 2 * i] for i in range(7))
     arr = scratch[16:18]
     stage = scratch[18:20]
     (
         weights, raw, sums, degs, scale, field, before,
-        pick_in, pick_s,
+        pick_in, pick_s, prev_ref, last_ref, src_ref,
+        quarter, joined, pieces, by_z, by_plane, total, elim, inverse, solver, solved, landed, pick_row,
         raw_sem, pick_send, pick_recv, pick_loc, z_send, z_recv, y_send, y_recv,
+        x_send, x_recv, a_send, a_recv, b_send, b_recv, c_send, c_recv, e_send, e_recv,
     ) = scratch[20:]
+    xi = lax.axis_index("col")
     me = lax.axis_index("blk")
     zi, yi, ci = me // 8, (me // 2) % NY, me % 2
     up = ((zi + 1) % NZ) * 8 + yi * 2 + ci
@@ -54,8 +53,23 @@
         return zi * 8 + ((yi + dy) % NY) * 2 + (ci + dc) % 2
 
     barrier = pltpu.get_barrier_semaphore()
-    for other in [up, down] + [partner(j) for j in range(1, 8)]:
-        pl.semaphore_signal(barrier, inc=1, device_id={"blk": other}, device_id_type=MESH)
+    for dz in range(1, NZ):
+        pl.semaphore_signal(
+            barrier, inc=1, device_id={"blk": (me + 8 * dz) % 64}, device_id_type=MESH
+        )
+
+    def plane_peer(m):
+        dx, dy, dc = m // 8, (m // 2) % NY, m % 2
+        return {
+            "blk": zi * 8 + ((yi + dy) % NY) * 2 + (ci + dc) % 2,
+            "col": (xi + dx) % NX,
+        }
+
+    def greet(m, carry):
+        pl.semaphore_signal(barrier, inc=1, device_id=plane_peer(m), device_id_type=MESH)
+        return carry
+
+    lax.fori_loop(1, PLANE, greet, 0)
 
     def raw_copies(k):
         return [
@@ -67,11 +81,14 @@
 
     for copy in raw_copies(0):
         copy.start()
-    pl.semaphore_wait(barrier, 9)
+    pl.semaphore_wait(barrier, NZ - 1 + PLANE - 1)
+
+    pick_row[...] = jnp.zeros((8, 128), jnp.int32)
+    pick_row[0:1, 0:64] = picks_ref[...]
 
     def pick_copy(j):
         return pltpu.make_async_remote_copy(
-            src_ref=picks_ref,
+            src_ref=pick_row,
             dst_ref=pick_in.at[j],
             send_sem=pick_send.at[j],
             recv_sem=pick_recv.at[j],
@@ -97,28 +114,51 @@
 
         def one(i, c):
             t = k * CHUNK + i
+            row, slot = rows_ref[t], slots_ref[t]
+            before_t = jnp.int32(0)
+            for q in range(RB):
+                last_q = last_ref[q]
+                before_t = jnp.where(row == q, last_q, before_t)
+                last_ref[q] = jnp.where(row == q, t + 1, last_q)
+            prev_ref[t] = before_t
+            owner = slot - RB
+            dz = (owner // 8 - zi + NZ) % NZ
+            place = jnp.where(dz < 4, 2 * dz, jnp.where(dz == 4, 7, 15 - 2 * dz))
+            j = ((yi - (owner // 2) % NY + NY) % NY) * 2 + (ci + owner) % 2
+            src_ref[t] = jnp.where(t < NEAR, slot, j * 8 + place)
             re_t = raw[k % 2, 0, i].T
             im_t = raw[k % 2, 1, i].T
             weights[t, 0:ORDER] = re_t
             weights[t, ORDER : 2 * ORDER] = im_t
             count = jnp.dot(ones, jnp.abs(re_t) + jnp.abs(im_t), preferred_element_type=jnp.float32)
-            degs[t + 1] = count + degs[prev_ref[t]]
+            degs[t + 1] = count + degs[before_t]
             return c
 
         return lax.fori_loop(0, CHUNK, one, carry, unroll=4)
 
+    for r in range(RB):
+        last_ref[r] = jnp.int32(0)
     lax.fori_loop(0, TILES // CHUNK, load_chunk, 0)
     for r in range(RB):
         scale[r] = 1.0 / jnp.sqrt(jnp.maximum(degs[last_ref[r]], 1.0))
 
-    pick_in[0] = picks_ref[...]
+    pick_in[0] = pick_row[...]
     for j in range(1, 8):
         pick_copy(j).wait()
     to_smem = pltpu.make_async_copy(pick_in, pick_s, pick_loc.at[0])
     to_smem.start()
     to_smem.wait()
 
-    field[...] = y_ref[...]
+    to_row = lax.broadcasted_iota(jnp.int32, (GROUP, GROUP), 0)
+    from_row = lax.broadcasted_iota(jnp.int32, (GROUP, GROUP), 1)
+    part_first = (from_row == (to_row % HALF) * 2 + to_row // HALF).astype(jnp.float32)
+    for r in range(RB):
+        field[r] = jnp.dot(
+            part_first,
+            y_ref[:, r * ORDER : (r + 1) * ORDER],
+            precision=lax.Precision.HIGHEST,
+            preferred_element_type=jnp.float32,
+        )
 
     def z_copy(par, way, hop, half):
         place_in = 2 * hop - 1 + way if hop > 0 else 0
@@ -210,11 +250,8 @@
             moved = ((1.0 - center) * now - sums[last_ref[r]] * s4) / half_width
             if step > 0:
                 moved = 2.0 * moved - before[r]
-            if step < STEPS - 1:
-                before[r] = now
-                field[r] = moved
-            else:
-                out_ref[r] = moved
+            before[r] = now
+            field[r] = moved
         for hop in range(4):
             for way in range(2):
                 for half in range(2):
@@ -224,31 +261,176 @@
             for j in range(1, 8):
                 y_copy(par, j, g).wait_send()
 
-
-def chebyshev(y_start, tile_real, tile_imag, tile_rows, tile_slots, fetch_pick):
-    me = lax.axis_index("blk")
-    zi, yi, ci = me // 8, (me // 2) % NY, me % 2
-    order = jnp.arange(TILES, dtype=jnp.int32)
-    same = (tile_rows[:, None] == tile_rows[None, :]) & (order[None, :] < order[:, None])
-    prev = jnp.max(jnp.where(same, order[None, :] + 1, 0), axis=1)
-    here = tile_rows[None, :] == jnp.arange(RB, dtype=jnp.int32)[:, None]
-    last = jnp.max(jnp.where(here, order[None, :] + 1, 0), axis=1)
-    owner = tile_slots - RB
-    zp, yp, cp = owner // 8, (owner // 2) % NY, owner % 2
-    dz = (zp - zi) % NZ
-    place = jnp.where(
-        dz == 0, 0, jnp.where(dz < 4, 2 * dz, jnp.where(dz == 4, 7, 2 * (8 - dz) - 1))
-    )
-    j = ((yi - yp) % NY) * 2 + (ci + cp) % 2
-    src = jnp.where(order < NEAR, tile_slots, j * 8 + place)
-    picks = jnp.pad(fetch_pick, ((0, 7), (0, 64)))
+    def x_copy(dx):
+        to = (xi + dx) % NX
+        return pltpu.make_async_remote_copy(
+            src_ref=field.at[pl.ds(to * 2, 2)],
+            dst_ref=quarter.at[xi],
+            send_sem=x_send.at[dx],
+            recv_sem=x_recv.at[dx],
+            device_id={"col": to},
+            device_id_type=MESH,
+        )
+
+    for dx in (2, 1, 3):
+        x_copy(dx).start()
+    quarter[xi] = field[pl.ds(xi * 2, 2)]
+    for dx in range(1, NX):
+        x_copy(dx).wait()
+    for b in range(2):
+        cols = slice(b * ORDER, (b + 1) * ORDER)
+        for q in range(NX):
+            joined[q * HALF : (q + 1) * HALF, cols] = quarter[q, b, 0:HALF]
+            joined[VEC + q * HALF : VEC + (q + 1) * HALF, cols] = quarter[q, b, HALF:GROUP]
+
+    gram = jnp.zeros((VEC, 2 * VEC), jnp.float32)
+    for b in range(2):
+        cols = slice(b * ORDER, (b + 1) * ORDER)
+        top, low = joined[0:VEC, cols], joined[VEC : 2 * VEC, cols]
+        right = jnp.concatenate(
+            [jnp.concatenate([top, low], axis=1), jnp.concatenate([-low, top], axis=1)], axis=0
+        )
+        gram += lax.dot_general(
+            jnp.concatenate([top, low], axis=1),
+            right,
+            (((1,), (1,)), ((), ())),
+            precision=lax.Precision.HIGHEST,
+            preferred_element_type=jnp.float32,
+        )
+    for i in range(8):
+        pieces[i] = gram[i * 8 : (i + 1) * 8]
+
+    def a_copy(dz):
+        to = (zi + dz) % NZ
+        return pltpu.make_async_remote_copy(
+            src_ref=pieces.at[to],
+            dst_ref=by_z.at[zi],
+            send_sem=a_send.at[dz],
+            recv_sem=a_recv.at[dz],
+            device_id={"blk": (me + 8 * dz) % 64},
+            device_id_type=MESH,
+        )
+
+    for dz in range(1, NZ):
+        a_copy(dz).start()
+    by_z[zi] = pieces[zi]
+    for dz in range(1, NZ):
+        a_copy(dz).wait()
+    mine = by_z[0]
+    for i in range(1, NZ):
+        mine += by_z[i]
+    place = xi * 8 + yi * 2 + ci
+    by_plane[place] = mine
+
+    def b_copy(m):
+        return pltpu.make_async_remote_copy(
+            src_ref=by_plane.at[place],
+            dst_ref=by_plane.at[place],
+            send_sem=b_send.at[m],
+            recv_sem=b_recv.at[m],
+            device_id=plane_peer(m),
+            device_id_type=MESH,
+        )
+
+    def b_start(m, carry):
+        b_copy(m).start()
+        return carry
+
+    def b_wait(m, carry):
+        b_copy(m).wait()
+        return carry
+
+    lax.fori_loop(1, PLANE, b_start, 0)
+    lax.fori_loop(1, PLANE, b_wait, 0)
+    mine = by_plane[0]
+    for i in range(1, PLANE):
+        mine += by_plane[i]
+    total[zi] = mine
+
+    def c_copy(dz):
+        return pltpu.make_async_remote_copy(
+            src_ref=total.at[zi],
+            dst_ref=total.at[zi],
+            send_sem=c_send.at[dz],
+            recv_sem=c_recv.at[dz],
+            device_id={"blk": (me + 8 * dz) % 64},
+            device_id_type=MESH,
+        )
+
+    for dz in range(1, NZ):
+        c_copy(dz).start()
+    for dz in range(1, NZ):
+        c_copy(dz).wait()
+
+    wide = (VEC, 2 * VEC)
+    sub = lax.broadcasted_iota(jnp.int32, wide, 0)
+    lane = lax.broadcasted_iota(jnp.int32, wide, 1)
+    sign = jnp.where(lane < VEC, -1.0, 1.0).astype(jnp.float32)
+    for i in range(8):
+        elim[i * 8 : (i + 1) * 8] = total[i]
+    inverse[...] = (lane == sub).astype(jnp.float32)
+
+    def eliminate(k, carry):
+        a, v = elim[...], inverse[...]
+        a_row = jnp.broadcast_to(elim[pl.ds(k, 1)], wide)
+        v_row = jnp.broadcast_to(inverse[pl.ds(k, 1)], wide)
+        pivot = jnp.sum(jnp.where(lane == k, a_row, 0.0), axis=1, keepdims=True)
+        col_re = jnp.sum(jnp.where(lane == k, a, 0.0), axis=1, keepdims=True)
+        col_im = jnp.sum(jnp.where(lane == k + VEC, a, 0.0), axis=1, keepdims=True)
+        below = sub > k
+        m_re = jnp.where(below, col_re / pivot, 0.0)
+        m_im = jnp.where(below, col_im / pivot, 0.0)
+        a_turned = pltpu.roll(a_row, VEC, 1) * sign
+        v_turned = pltpu.roll(v_row, VEC, 1) * sign
+        elim[...] = a - m_re * a_row - m_im * a_turned
+        inverse[...] = v - m_re * v_row - m_im * v_turned
+        return carry
+
+    lax.fori_loop(0, VEC, eliminate, 0)
+    pivots = jnp.sum(jnp.where(lane == sub, elim[...], 0.0), axis=1, keepdims=True)
+    scaled = inverse[...] * (math.sqrt(NODES) / jnp.sqrt(pivots))
+    solver[pl.ds(0, VEC, stride=2), :] = -sign * scaled
+    solver[pl.ds(1, VEC, stride=2), :] = pltpu.roll(scaled, VEC, 1)
+
+    def e_copy(dx):
+        to = (xi + dx) % NX
+        return pltpu.make_async_remote_copy(
+            src_ref=solved.at[to],
+            dst_ref=landed.at[xi],
+            send_sem=e_send.at[dx],
+            recv_sem=e_recv.at[dx],
+            device_id={"col": to},
+            device_id_type=MESH,
+        )
+
+    for dx in (2, 1, 3, 0):
+        to = (xi + dx) % NX
+        part = jnp.dot(
+            solver[pl.ds(to * GROUP, GROUP)],
+            joined[...],
+            precision=lax.Precision.HIGHEST,
+            preferred_element_type=jnp.float32,
+        )
+        if dx:
+            solved[to] = part
+            e_copy(dx).start()
+        else:
+            landed[xi] = part
+    for dx in range(1, NX):
+        e_copy(dx).wait()
+    for q in range(NX):
+        out_ref[:, q * 512 : (q + 1) * 512] = landed[q]
+
+
+def per_device(y_start, tile_real, tile_imag, tile_rows, tile_slots, fetch_pick):
     block = (RB, GROUP, ORDER)
-    split = y_start.reshape(HALF, 2, RB, ORDER).transpose(2, 1, 0, 3).reshape(block)
-    done = pl.pallas_call(
+    tiny = (8, 8, 128)
+    dma = pltpu.SemaphoreType.DMA
+    return pl.pallas_call(
         filter_kernel,
         name="filter",
-        out_shape=jax.ShapeDtypeStruct(block, jnp.float32),
-        in_specs=[pl.BlockSpec(memory_space=pltpu.SMEM)] * 3
+        out_shape=jax.ShapeDtypeStruct(y_start.shape, jnp.float32),
+        in_specs=[pl.BlockSpec(memory_space=pltpu.SMEM)] * 2
         + [pl.BlockSpec(memory_space=pltpu.VMEM)] * 2
         + [pl.BlockSpec(memory_space=pl.ANY)] * 2,
         out_specs=pl.BlockSpec(memory_space=pltpu.VMEM),
@@ -264,34 +446,44 @@
             pltpu.VMEM(block, jnp.float32),
             pltpu.VMEM((8, 8, 128), jnp.int32),
             pltpu.SMEM((8, 8, 128), jnp.int32),
-            pltpu.SemaphoreType.DMA((2, 2)),
-            pltpu.SemaphoreType.DMA((8,)),
-            pltpu.SemaphoreType.DMA((8,)),
-            pltpu.SemaphoreType.DMA((1,)),
-            pltpu.SemaphoreType.DMA((2, 2, 4, 2)),
-            pltpu.SemaphoreType.DMA((2, 2, 4, 2)),
-            pltpu.SemaphoreType.DMA((2, 8, 5)),
-            pltpu.SemaphoreType.DMA((2, 8, 5)),
+            pltpu.SMEM((TILES,), jnp.int32),
+            pltpu.SMEM((RB,), jnp.int32),
+            pltpu.SMEM((TILES,), jnp.int32),
+            pltpu.VMEM((NX, 2, GROUP, ORDER), jnp.float32),
+            pltpu.VMEM((2 * VEC, 512), jnp.float32),
+            pltpu.VMEM(tiny, jnp.float32),
+            pltpu.VMEM(tiny, jnp.float32),
+            pltpu.VMEM((PLANE, 8, 128), jnp.float32),
+            pltpu.VMEM(tiny, jnp.float32),
+            pltpu.VMEM((VEC, 2 * VEC), jnp.float32),
+            pltpu.VMEM((VEC, 2 * VEC), jnp.float32),
+            pltpu.VMEM((2 * VEC, 2 * VEC), jnp.float32),
+            pltpu.VMEM((NX, GROUP, 512), jnp.float32),
+            pltpu.VMEM((NX, GROUP, 512), jnp.float32),
+            pltpu.VMEM((8, 128), jnp.int32),
+            dma((2, 2)),
+            dma((8,)),
+            dma((8,)),
+            dma((1,)),
+            dma((2, 2, 4, 2)),
+            dma((2, 2, 4, 2)),
+            dma((2, 8, 5)),
+            dma((2, 8, 5)),
+            dma((NX,)),
+            dma((NX,)),
+            dma((NZ,)),
+            dma((NZ,)),
+            dma((PLANE,)),
+            dma((PLANE,)),
+            dma((NZ,)),
+            dma((NZ,)),
+            dma((NX,)),
+            dma((NX,)),
         ],
         compiler_params=pltpu.CompilerParams(
-            collective_id=0, has_side_effects=True, vmem_limit_bytes=58 << 20
+            collective_id=0, has_side_effects=True, vmem_limit_bytes=60 << 20
         ),
-    )(prev, last, src, split, picks, tile_real, tile_imag)
-    return done.reshape(RB, 2, HALF, ORDER).transpose(2, 1, 0, 3).reshape(y_start.shape)
-
-
-def per_device(y_start, tile_real, tile_imag, tile_rows, tile_slots, fetch_pick):
-    group, rows = y_start.shape
-    nblk = lax.axis_size("blk")
-    current = chebyshev(y_start, tile_real, tile_imag, tile_rows, tile_slots, fetch_pick)
-    gathered = lax.all_gather(current, "col", axis=0, tiled=True)
-    partial_gram = jnp.dot(gathered, gathered.T, precision=lax.Precision.HIGHEST)
-    gram = lax.psum(partial_gram, "blk")
-    gram = gram + turn(turn(gram).T).T
-    lower = jnp.linalg.cholesky(gram)
-    solved = jax.scipy.linalg.solve_triangular(lower, gathered, lower=True)
-    mine = lax.dynamic_slice_in_dim(solved, lax.axis_index("col") * group, group, 0)
-    return mine * math.sqrt(rows * nblk)
+    )(tile_rows, tile_slots, y_start, fetch_pick, tile_real, tile_imag)
 
 
 def solution(mesh):

time: 375 us -> 166 us (0.44)
  waiting for transfers between devices: 192 us -> 0 us
  Pallas kernels: 129 us -> 164 us
  other arithmetic: 28.7 us -> 0 us
  between operations: 13.5 us -> 0.01 us
  matrix products: 5.43 us -> 0 us
  local copies, waits for them, and re-layouts: 6.14 us -> 1.67 us
    psum x1 -> x0, waiting for transfers between devices: 169 us -> none  [per_device(): gram = lax.psum(partial_gram, 'blk')]
    pallas_call x1, Pallas kernels: 129 us -> 164 us  [per_device(): pl.pallas_call(filter_kernel, name='filter', out_shape=jax.ShapeDtypeStru...]
    another operation x7 -> x0, other arithmetic: 23 us -> none  [the longest x3 12.4 us: per_device(): lower = jnp.linalg.cholesky(gram)]
    all_gather x1 -> x0, waiting for transfers between devices: 22.7 us -> none  [per_device(): gathered = lax.all_gather(current, 'col', axis=0, tiled=True)]
  transfers between devices with their start and end apart: 2 -> 0, of which waited for: 2 -> 0; matrix products, arithmetic and copies ran while one was open for 0% -> 0% of each run, Pallas kernels for 0% -> 0%
where the time goes in v2:
time: 166 us
  Pallas kernels  164 us (99%)
  local copies, waits for them, and re-layouts  1.67 us (1%)
    pallas_call x1, Pallas kernels, per_device(): pl.pallas_call(filter_kernel, name='filter', out_shape=jax.ShapeDtypeStru...  164 us

profile of v2, /device:TPU:1, one launch (start us, length us, event | category | flops | bytes accessed | tf_op | source)
XLA Modules:
  0.0 166.2 jit_solution(1139172937562194421)
XLA Ops:
  0.0 164.5 %filter.1 = f32[32,2048]{1,0:T(8,128)} custom-call(s32[96]{0:T(128)} %rows_ref.1, s32[96]{0:T(128)} %slots_ref.1, f32[32,2048]{1,0:T(8,128)} %y_ref.1, s32[1,64]{1,0:T(1,128)} %picks_ref.1, bf16[96,256,256]{2,1,0:T(8,128)(2,1)} %real_ref.1, bf16[96,256,256]{2,1,0:T(8,128)(2,1)} %imag_ref.1), custom_call_target="tpu_custom_call" | custom-call | tf_op jit(solution)/shard_map/filter/pallas_call | solution.py:429
  164.5 1.7 %copy.8 = f32[32,2048]{1,0:T(8,128)} copy(f32[32,2048]{1,0:T(8,128)} %filter.1) | data formatting | bytes 524288

commit v3 on v2

--- a/solution.py
+++ b/solution.py
@@ -27,36 +27,43 @@
 
 Z_PLACE = (0, 2, 4, 6, 7, 5, 3, 1)
 Z_OFFSET = (0, 7, 1, 6, 2, 5, 3, 4)
-GROUPS = ((0, 1), (1, 2), (3, 2), (5, 2), (7, 1))
+GROUPS = ((0, 1), (1, 2), (3, 2))
 
 
 def filter_kernel(rows_ref, slots_ref, y_ref, picks_ref, real_ref, imag_ref, out_ref, *scratch):
     own = scratch[0:2]
-    zbuf = (None,) + tuple(scratch[2 + 2 * i : 4 + 2 * i] for i in range(7))
-    arr = scratch[16:18]
-    stage = scratch[18:20]
+    zbuf = (None,) + tuple(scratch[2 + 2 * i : 4 + 2 * i] for i in range(4))
+    arr = scratch[10:12]
+    stage = scratch[12:14]
+    away = scratch[14:16]
     (
         weights, raw, sums, degs, scale, field, before,
         pick_in, pick_s, prev_ref, last_ref, src_ref,
         quarter, joined, pieces, by_z, by_plane, total, elim, inverse, solver, solved, landed, pick_row,
-        raw_sem, pick_send, pick_recv, pick_loc, z_send, z_recv, y_send, y_recv,
+        raw_sem, pick_send, pick_recv, pick_loc, z_send, z_recv, y_send, y_recv, w_send, w_recv,
         x_send, x_recv, a_send, a_recv, b_send, b_recv, c_send, c_recv, e_send, e_recv,
-    ) = scratch[20:]
+    ) = scratch[16:]
     xi = lax.axis_index("col")
     me = lax.axis_index("blk")
     zi, yi, ci = me // 8, (me // 2) % NY, me % 2
-    up = ((zi + 1) % NZ) * 8 + yi * 2 + ci
-    down = ((zi + NZ - 1) % NZ) * 8 + yi * 2 + ci
+    def device(dz, dy, dc):
+        return ((zi + dz + NZ) % NZ) * 8 + ((yi + dy + NY) % NY) * 2 + (ci + dc) % 2
 
     def partner(j):
-        dy, dc = j // 2, j % 2
-        return zi * 8 + ((yi + dy) % NY) * 2 + (ci + dc) % 2
+        return device(0, j // 2, j % 2)
+
+    def reader(q):
+        if q < 8:
+            return 0, q // 2, q % 2
+        if q < 24:
+            return (1 if q < 16 else -1), (q % 8) // 2, q % 2
+        return (2, q - 24, 0) if q < 28 else (-2, q - 28, 1)
 
     barrier = pltpu.get_barrier_semaphore()
-    for dz in range(1, NZ):
-        pl.semaphore_signal(
-            barrier, inc=1, device_id={"blk": (me + 8 * dz) % 64}, device_id_type=MESH
-        )
+    others = [(dz, j // 2, j % 2) for dz in (1, -1, 2, -2) for j in range(8)]
+    others += [(dz, 0, 0) for dz in (3, 4, -3)]
+    for other in others:
+        pl.semaphore_signal(barrier, inc=1, device_id={"blk": device(*other)}, device_id_type=MESH)
 
     def plane_peer(m):
         dx, dy, dc = m // 8, (m // 2) % NY, m % 2
@@ -81,23 +88,19 @@
 
     for copy in raw_copies(0):
         copy.start()
-    pl.semaphore_wait(barrier, NZ - 1 + PLANE - 1)
-
-    pick_row[...] = jnp.zeros((8, 128), jnp.int32)
+    pick_row[...] = jnp.zeros((1, 128), jnp.int32)
     pick_row[0:1, 0:64] = picks_ref[...]
 
-    def pick_copy(j):
+    def pick_copy(q):
+        dz, dy, dc = reader(q)
         return pltpu.make_async_remote_copy(
             src_ref=pick_row,
-            dst_ref=pick_in.at[j],
-            send_sem=pick_send.at[j],
-            recv_sem=pick_recv.at[j],
-            device_id={"blk": partner(j)},
-            device_id_type=MESH,
-        )
-
-    for j in range(1, 8):
-        pick_copy(j).start()
+            dst_ref=pick_in.at[q],
+            send_sem=pick_send.at[q],
+            recv_sem=pick_recv.at[q],
+            device_id={"blk": device(-dz, -dy, dc)},
+            device_id_type=MESH,
+        )
 
     degs[0] = jnp.zeros((8, ORDER), jnp.float32)
     sums[0] = jnp.zeros((GROUP, ORDER), jnp.float32)
@@ -134,17 +137,21 @@
             degs[t + 1] = count + degs[before_t]
             return c
 
-        return lax.fori_loop(0, CHUNK, one, carry, unroll=4)
+        return lax.fori_loop(0, CHUNK, one, carry, unroll=CHUNK)
 
     for r in range(RB):
         last_ref[r] = jnp.int32(0)
-    lax.fori_loop(0, TILES // CHUNK, load_chunk, 0)
+    lax.fori_loop(0, TILES // CHUNK // 2, load_chunk, 0)
+    pl.semaphore_wait(barrier, len(others) + PLANE - 1)
+    for q in range(1, 32):
+        pick_copy(q).start()
+    lax.fori_loop(TILES // CHUNK // 2, TILES // CHUNK, load_chunk, 0)
     for r in range(RB):
         scale[r] = 1.0 / jnp.sqrt(jnp.maximum(degs[last_ref[r]], 1.0))
 
     pick_in[0] = pick_row[...]
-    for j in range(1, 8):
-        pick_copy(j).wait()
+    for q in range(1, 32):
+        pick_copy(q).wait()
     to_smem = pltpu.make_async_copy(pick_in, pick_s, pick_loc.at[0])
     to_smem.start()
     to_smem.wait()
@@ -160,17 +167,26 @@
             preferred_element_type=jnp.float32,
         )
 
-    def z_copy(par, way, hop, half):
-        place_in = 2 * hop - 1 + way if hop > 0 else 0
-        place_out = 2 * hop + 1 + way if hop < 3 else 7
-        source = own[par] if hop == 0 else zbuf[place_in][par]
+    def z_copy(par, way, kind, half):
+        source = own[par] if kind == 0 else zbuf[1 + way][par]
         part = pl.ds(half * 4, 4)
         return pltpu.make_async_remote_copy(
             src_ref=source.at[part],
-            dst_ref=zbuf[place_out][par].at[part],
-            send_sem=z_send.at[par, way, hop, half],
-            recv_sem=z_recv.at[par, way, hop, half],
-            device_id={"blk": down if way else up},
+            dst_ref=zbuf[1 + 2 * kind + way][par].at[part],
+            send_sem=z_send.at[par, way, kind, half],
+            recv_sem=z_recv.at[par, way, kind, half],
+            device_id={"blk": device(-1 if way else 1, 0, 0)},
+            device_id_type=MESH,
+        )
+
+    def w_copy(par, q):
+        dz, dy, dc = reader(q)
+        return pltpu.make_async_remote_copy(
+            src_ref=away[par].at[q - 8],
+            dst_ref=arr[par].at[dy * 2 + dc, 5 if dz == 1 else 6 if dz == -1 else 7],
+            send_sem=w_send.at[par, q - 8],
+            recv_sem=w_recv.at[par, q - 8],
+            device_id={"blk": device(dz, dy, dc)},
             device_id_type=MESH,
         )
 
@@ -193,8 +209,7 @@
             for k in range(first, first + count):
                 source = own[par] if k == 0 else zbuf[k][par]
                 owner = ((zi + Z_OFFSET[k]) % NZ) * 8 + yi * 2 + ci
-                row = ((4 - j // 2) % 4) * 2 + j % 2
-                block = source[pick_s[row, 0, owner]]
+                block = source[pick_s[j, 0, owner]]
                 if j == 0:
                     arr[par][0, k] = block
                 else:
@@ -209,8 +224,9 @@
             left, weights[t], preferred_element_type=jnp.float32
         )
 
-    for step in range(STEPS):
-        par = step % 2
+    before[...] = jnp.zeros_like(before)
+
+    def apply(par, factor):
         for r in range(RB):
             s4 = jnp.concatenate([scale[r]] * 4, axis=0)
             own[par][r] = (field[r] * s4).astype(jnp.bfloat16)
@@ -224,19 +240,27 @@
             return c
 
         lax.fori_loop(0, NEAR, near, 0, unroll=UNROLL)
-        for hop in range(1, 4):
-            for half in range(2):
+        for half in range(2):
+            for way in range(2):
+                z_copy(par, way, 0, half).wait_recv()
+                z_copy(par, way, 1, half).start()
+        hand_on(par, 1)
+        for half in range(2):
+            for way in range(2):
+                z_copy(par, way, 1, half).wait_recv()
+        for first in (24, 8):
+            for i in range(4 if first == 24 else 8):
                 for way in range(2):
-                    z_copy(par, way, hop - 1, half).wait_recv()
-                    if hop < 3 or half == way:
-                        z_copy(par, way, hop, half).start()
-            hand_on(par, hop)
-        for way in range(2):
-            z_copy(par, way, 3, way).wait_recv()
-        hand_on(par, 4)
-        for g in range(5):
+                    q = first + way * (4 if first == 24 else 8) + i
+                    owner = device(2 if way else -2, 0, 0)
+                    away[par][q - 8] = zbuf[3 + way][par][pick_s[q, 0, owner]]
+                    w_copy(par, q).start()
+        hand_on(par, 2)
+        for g in range(3):
             for j in range(1, 8):
                 y_copy(par, j, g).wait_recv()
+        for q in range(8, 32):
+            w_copy(par, q).wait_recv()
 
         def far(t, c):
             place = src_ref[t]
@@ -248,18 +272,24 @@
             s4 = jnp.concatenate([scale[r]] * 4, axis=0)
             now = field[r]
             moved = ((1.0 - center) * now - sums[last_ref[r]] * s4) / half_width
-            if step > 0:
-                moved = 2.0 * moved - before[r]
+            field[r] = factor * moved - before[r]
             before[r] = now
-            field[r] = moved
-        for hop in range(4):
+        for kind in range(2):
             for way in range(2):
                 for half in range(2):
-                    if hop < 3 or half == way:
-                        z_copy(par, way, hop, half).wait_send()
-        for g in range(5):
+                    z_copy(par, way, kind, half).wait_send()
+        for g in range(3):
             for j in range(1, 8):
                 y_copy(par, j, g).wait_send()
+        for q in range(8, 32):
+            w_copy(par, q).wait_send()
+
+    def two_steps(i, c):
+        apply(0, jnp.where(i == 0, 1.0, 2.0).astype(jnp.float32))
+        apply(1, 2.0)
+        return c
+
+    lax.fori_loop(0, STEPS // 2, two_steps, 0)
 
     def x_copy(dx):
         to = (xi + dx) % NX
@@ -434,8 +464,9 @@
         + [pl.BlockSpec(memory_space=pltpu.VMEM)] * 2
         + [pl.BlockSpec(memory_space=pl.ANY)] * 2,
         out_specs=pl.BlockSpec(memory_space=pltpu.VMEM),
-        scratch_shapes=[pltpu.VMEM(block, jnp.bfloat16)] * 16
+        scratch_shapes=[pltpu.VMEM(block, jnp.bfloat16)] * 10
         + [pltpu.VMEM((8,) + block, jnp.bfloat16)] * 4
+        + [pltpu.VMEM((24,) + block[1:], jnp.bfloat16)] * 2
         + [
             pltpu.VMEM((TILES, 2 * ORDER, ORDER), jnp.bfloat16),
             pltpu.VMEM((2, 2, CHUNK, ORDER, ORDER), jnp.bfloat16),
@@ -444,8 +475,8 @@
             pltpu.VMEM((RB, 8, ORDER), jnp.float32),
             pltpu.VMEM(block, jnp.float32),
             pltpu.VMEM(block, jnp.float32),
-            pltpu.VMEM((8, 8, 128), jnp.int32),
-            pltpu.SMEM((8, 8, 128), jnp.int32),
+            pltpu.VMEM((32, 1, 128), jnp.int32),
+            pltpu.SMEM((32, 1, 128), jnp.int32),
             pltpu.SMEM((TILES,), jnp.int32),
             pltpu.SMEM((RB,), jnp.int32),
             pltpu.SMEM((TILES,), jnp.int32),
@@ -460,15 +491,17 @@
             pltpu.VMEM((2 * VEC, 2 * VEC), jnp.float32),
             pltpu.VMEM((NX, GROUP, 512), jnp.float32),
             pltpu.VMEM((NX, GROUP, 512), jnp.float32),
-            pltpu.VMEM((8, 128), jnp.int32),
+            pltpu.VMEM((1, 128), jnp.int32),
             dma((2, 2)),
-            dma((8,)),
-            dma((8,)),
+            dma((32,)),
+            dma((32,)),
             dma((1,)),
-            dma((2, 2, 4, 2)),
-            dma((2, 2, 4, 2)),
-            dma((2, 8, 5)),
-            dma((2, 8, 5)),
+            dma((2, 2, 2, 2)),
+            dma((2, 2, 2, 2)),
+            dma((2, 8, 3)),
+            dma((2, 8, 3)),
+            dma((2, 24)),
+            dma((2, 24)),
             dma((NX,)),
             dma((NX,)),
             dma((NZ,)),

time: 166 us -> 154 us (0.928)
  Pallas kernels: 164 us -> 152 us
    pallas_call x1, Pallas kernels: 164 us -> 152 us  [per_device(): pl.pallas_call(filter_kernel, name='filter', out_shape=jax.ShapeDtypeStru...]
where the time goes in v3:
time: 154 us; the launch traced here: 153 us
  Pallas kernels  152 us (99%)
  local copies, waits for them, and re-layouts  1.67 us (1%)
    pallas_call x1, Pallas kernels, per_device(): pl.pallas_call(filter_kernel, name='filter', out_shape=jax.ShapeDtypeStru...  152 us

profile of v3, /device:TPU:1, one launch (start us, length us, event | category | flops | bytes accessed | tf_op | source)
XLA Modules:
  0.0 153.4 jit_solution(6664040034104314510)
XLA Ops:
  0.0 151.7 %filter.1 = f32[32,2048]{1,0:T(8,128)} custom-call(s32[96]{0:T(128)} %rows_ref.1, s32[96]{0:T(128)} %slots_ref.1, f32[32,2048]{1,0:T(8,128)} %y_ref.1, s32[1,64]{1,0:T(1,128)} %picks_ref.1, bf16[96,256,256]{2,1,0:T(8,128)(2,1)} %real_ref.1, bf16[96,256,256]{2,1,0:T(8,128)(2,1)} %imag_ref.1), custom_call_target="tpu_custom_call" | custom-call | tf_op jit(solution)/shard_map/filter/pallas_call | solution.py:459
  151.7 1.7 %copy.8 = f32[32,2048]{1,0:T(8,128)} copy(f32[32,2048]{1,0:T(8,128)} %filter.1) | data formatting | bytes 524288

commit v4 on v3

--- a/solution.py
+++ b/solution.py
@@ -46,8 +46,15 @@
     xi = lax.axis_index("col")
     me = lax.axis_index("blk")
     zi, yi, ci = me // 8, (me // 2) % NY, me % 2
+    ids = {
+        (dz, dy, dc): ((zi + dz) % NZ) * 8 + ((yi + dy) % NY) * 2 + (ci + dc) % 2
+        for dz in range(NZ)
+        for dy in range(NY)
+        for dc in range(2)
+    }
+
     def device(dz, dy, dc):
-        return ((zi + dz + NZ) % NZ) * 8 + ((yi + dy + NY) % NY) * 2 + (ci + dc) % 2
+        return ids[dz % NZ, dy % NY, dc % 2]
 
     def partner(j):
         return device(0, j // 2, j % 2)
@@ -169,7 +176,7 @@
 
     def z_copy(par, way, kind, half):
         source = own[par] if kind == 0 else zbuf[1 + way][par]
-        part = pl.ds(half * 4, 4)
+        part = pl.ds(half * 2, 2)
         return pltpu.make_async_remote_copy(
             src_ref=source.at[part],
             dst_ref=zbuf[1 + 2 * kind + way][par].at[part],
@@ -208,7 +215,7 @@
                 continue
             for k in range(first, first + count):
                 source = own[par] if k == 0 else zbuf[k][par]
-                owner = ((zi + Z_OFFSET[k]) % NZ) * 8 + yi * 2 + ci
+                owner = device(Z_OFFSET[k], 0, 0)
                 block = source[pick_s[j, 0, owner]]
                 if j == 0:
                     arr[par][0, k] = block
@@ -230,7 +237,7 @@
         for r in range(RB):
             s4 = jnp.concatenate([scale[r]] * 4, axis=0)
             own[par][r] = (field[r] * s4).astype(jnp.bfloat16)
-        for half in range(2):
+        for half in range(4):
             for way in range(2):
                 z_copy(par, way, 0, half).start()
         hand_on(par, 0)
@@ -240,12 +247,12 @@
             return c
 
         lax.fori_loop(0, NEAR, near, 0, unroll=UNROLL)
-        for half in range(2):
+        for half in range(4):
             for way in range(2):
                 z_copy(par, way, 0, half).wait_recv()
                 z_copy(par, way, 1, half).start()
         hand_on(par, 1)
-        for half in range(2):
+        for half in range(4):
             for way in range(2):
                 z_copy(par, way, 1, half).wait_recv()
         for first in (24, 8):
@@ -256,6 +263,15 @@
                     away[par][q - 8] = zbuf[3 + way][par][pick_s[q, 0, owner]]
                     w_copy(par, q).start()
         hand_on(par, 2)
+        for kind in range(2):
+            for way in range(2):
+                for half in range(4):
+                    z_copy(par, way, kind, half).wait_send()
+        for g in range(3):
+            for j in range(1, 8):
+                y_copy(par, j, g).wait_send()
+        for q in range(8, 32):
+            w_copy(par, q).wait_send()
         for g in range(3):
             for j in range(1, 8):
                 y_copy(par, j, g).wait_recv()
@@ -267,22 +283,13 @@
             product(arr[par][place // 8, place % 8], t)
             return c
 
-        lax.fori_loop(NEAR, TILES, far, 0, unroll=UNROLL)
+        lax.fori_loop(NEAR, TILES, far, 0, unroll=40)
         for r in range(RB):
             s4 = jnp.concatenate([scale[r]] * 4, axis=0)
             now = field[r]
             moved = ((1.0 - center) * now - sums[last_ref[r]] * s4) / half_width
             field[r] = factor * moved - before[r]
             before[r] = now
-        for kind in range(2):
-            for way in range(2):
-                for half in range(2):
-                    z_copy(par, way, kind, half).wait_send()
-        for g in range(3):
-            for j in range(1, 8):
-                y_copy(par, j, g).wait_send()
-        for q in range(8, 32):
-            w_copy(par, q).wait_send()
 
     def two_steps(i, c):
         apply(0, jnp.where(i == 0, 1.0, 2.0).astype(jnp.float32))
@@ -370,8 +377,8 @@
         b_copy(m).wait()
         return carry
 
-    lax.fori_loop(1, PLANE, b_start, 0)
-    lax.fori_loop(1, PLANE, b_wait, 0)
+    lax.fori_loop(1, PLANE, b_start, 0, unroll=31)
+    lax.fori_loop(1, PLANE, b_wait, 0, unroll=31)
     mine = by_plane[0]
     for i in range(1, PLANE):
         mine += by_plane[i]
@@ -496,8 +503,8 @@
             dma((32,)),
             dma((32,)),
             dma((1,)),
-            dma((2, 2, 2, 2)),
-            dma((2, 2, 2, 2)),
+            dma((2, 2, 2, 4)),
+            dma((2, 2, 2, 4)),
             dma((2, 8, 3)),
             dma((2, 8, 3)),
             dma((2, 24)),

time: 154 us -> 150 us (0.974)
  Pallas kernels: 152 us -> 148 us
    pallas_call x1, Pallas kernels: 152 us -> 148 us  [per_device(): pl.pallas_call(filter_kernel, name='filter', out_shape=jax.ShapeDtypeStru...]
where the time goes in v4:
time: 150 us
  Pallas kernels  148 us (99%)
  local copies, waits for them, and re-layouts  1.67 us (1%)
    pallas_call x1, Pallas kernels, per_device(): pl.pallas_call(filter_kernel, name='filter', out_shape=jax.ShapeDtypeStru...  148 us

profile of v4, /device:TPU:1, one launch (start us, length us, event | category | flops | bytes accessed | tf_op | source)
XLA Modules:
  0.0 150.1 jit_solution(5594428463657336080)
XLA Ops:
  0.0 148.4 %filter.1 = f32[32,2048]{1,0:T(8,128)} custom-call(s32[96]{0:T(128)} %rows_ref.1, s32[96]{0:T(128)} %slots_ref.1, f32[32,2048]{1,0:T(8,128)} %y_ref.1, s32[1,64]{1,0:T(1,128)} %picks_ref.1, bf16[96,256,256]{2,1,0:T(8,128)(2,1)} %real_ref.1, bf16[96,256,256]{2,1,0:T(8,128)(2,1)} %imag_ref.1), custom_call_target="tpu_custom_call" | custom-call | tf_op jit(solution)/shard_map/filter/pallas_call | solution.py:466
  148.4 1.7 %copy.8 = f32[32,2048]{1,0:T(8,128)} copy(f32[32,2048]{1,0:T(8,128)} %filter.1) | data formatting | bytes 524288

commit v5 on v4

--- a/solution.py
+++ b/solution.py
@@ -407,23 +407,41 @@
         elim[i * 8 : (i + 1) * 8] = total[i]
     inverse[...] = (lane == sub).astype(jnp.float32)
 
-    def eliminate(k, carry):
+    lane_row, sign_row = lane[0:1], sign[0:1]
+
+    def entry(row, index):
+        return jnp.sum(jnp.where(lane_row == index, row, 0.0), axis=1, keepdims=True)
+
+    def column(matrix, index):
+        return jnp.sum(jnp.where(lane == index, matrix, 0.0), axis=1, keepdims=True)
+
+    def times_i(row):
+        return pltpu.roll(row, VEC, 1) * sign_row
+
+    def eliminate(i, carry):
+        k = 2 * i
         a, v = elim[...], inverse[...]
-        a_row = jnp.broadcast_to(elim[pl.ds(k, 1)], wide)
-        v_row = jnp.broadcast_to(inverse[pl.ds(k, 1)], wide)
-        pivot = jnp.sum(jnp.where(lane == k, a_row, 0.0), axis=1, keepdims=True)
-        col_re = jnp.sum(jnp.where(lane == k, a, 0.0), axis=1, keepdims=True)
-        col_im = jnp.sum(jnp.where(lane == k + VEC, a, 0.0), axis=1, keepdims=True)
-        below = sub > k
-        m_re = jnp.where(below, col_re / pivot, 0.0)
-        m_im = jnp.where(below, col_im / pivot, 0.0)
-        a_turned = pltpu.roll(a_row, VEC, 1) * sign
-        v_turned = pltpu.roll(v_row, VEC, 1) * sign
-        elim[...] = a - m_re * a_row - m_im * a_turned
-        inverse[...] = v - m_re * v_row - m_im * v_turned
+        a0, a1 = elim[pl.ds(k, 1)], elim[pl.ds(k + 1, 1)]
+        v0, v1 = inverse[pl.ds(k, 1)], inverse[pl.ds(k + 1, 1)]
+        inv0 = 1.0 / entry(a0, k)
+        g_re, g_im = entry(a1, k) * inv0, entry(a1, k + VEC) * inv0
+        e_re, e_im = entry(a0, k + 1), entry(a0, k + 1 + VEC)
+        inv1 = 1.0 / (entry(a1, k + 1) - (g_re * e_re - g_im * e_im))
+        a0_i, v0_i = times_i(a0), times_i(v0)
+        a1 = a1 - g_re * a0 - g_im * a0_i
+        v1 = v1 - g_re * v0 - g_im * v0_i
+        a1_i, v1_i = times_i(a1), times_i(v1)
+        m0_re = jnp.where(sub > k, column(a, k) * inv0, 0.0)
+        m0_im = jnp.where(sub > k, column(a, k + VEC) * inv0, 0.0)
+        c_re = column(a, k + 1) - (m0_re * e_re - m0_im * e_im)
+        c_im = column(a, k + 1 + VEC) - (m0_re * e_im + m0_im * e_re)
+        m1_re = jnp.where(sub > k + 1, c_re * inv1, 0.0)
+        m1_im = jnp.where(sub > k + 1, c_im * inv1, 0.0)
+        elim[...] = a - m0_re * a0 - m0_im * a0_i - m1_re * a1 - m1_im * a1_i
+        inverse[...] = v - m0_re * v0 - m0_im * v0_i - m1_re * v1 - m1_im * v1_i
         return carry
 
-    lax.fori_loop(0, VEC, eliminate, 0)
+    lax.fori_loop(0, VEC // 2, eliminate, 0)
     pivots = jnp.sum(jnp.where(lane == sub, elim[...], 0.0), axis=1, keepdims=True)
     scaled = inverse[...] * (math.sqrt(NODES) / jnp.sqrt(pivots))
     solver[pl.ds(0, VEC, stride=2), :] = -sign * scaled

time: 150 us -> 149 us (level)
  no operation moved by 1% of the time
where the time goes in v5:
time: 149 us
  Pallas kernels  147 us (99%)
  local copies, waits for them, and re-layouts  1.67 us (1%)
    pallas_call x1, Pallas kernels, per_device(): pl.pallas_call(filter_kernel, name='filter', out_shape=jax.ShapeDtypeStru...  147 us

profile of v5, /device:TPU:1, one launch (start us, length us, event | category | flops | bytes accessed | tf_op | source)
XLA Modules:
  0.0 148.8 jit_solution(5909974657270722697)
XLA Ops:
  0.0 147.1 %filter.1 = f32[32,2048]{1,0:T(8,128)} custom-call(s32[96]{0:T(128)} %rows_ref.1, s32[96]{0:T(128)} %slots_ref.1, f32[32,2048]{1,0:T(8,128)} %y_ref.1, s32[1,64]{1,0:T(1,128)} %picks_ref.1, bf16[96,256,256]{2,1,0:T(8,128)(2,1)} %real_ref.1, bf16[96,256,256]{2,1,0:T(8,128)(2,1)} %imag_ref.1), custom_call_target="tpu_custom_call" | custom-call | tf_op jit(solution)/shard_map/filter/pallas_call | solution.py:484
  147.1 1.7 %copy.8 = f32[32,2048]{1,0:T(8,128)} copy(f32[32,2048]{1,0:T(8,128)} %filter.1) | data formatting | bytes 524288
